TPU v7x, 256 devices: a whole 4x4x8 slice. The times are simulated.
256 devices in a mesh: wide: 32 (over y, z_lo, core), narrow: 8 (over z_hi, x).
Axes of the slice: x: 4, y: 4, z: 8 (z_hi: 2, z_lo: 4; z = z_hi * 4 + z_lo), core: 2. Of those that a mesh axis runs over, the one named last changes fastest.
Arguments:
- state: float32 [2, 33554432], P(None, ('wide', 'narrow')), may hold values from -6 to 6
- gate_re: float32 [6, 128, 128], replicated, may hold values from -0.375 to 0.375
- gate_im: float32 [6, 128, 128], replicated, may hold values from -0.375 to 0.375
- bit_orders: int32 [6, 8], replicated, may hold values from 0 to 7, each once within a row
- phase_pairs: int32 [6, 16, 2], replicated, may hold values from 0 to 11
- phase_angles: float32 [6, 16], replicated, may hold values from -3.140625 to 3.140625
Outputs:
- final_state: float32 [2, 33554432], P(None, ('wide', 'narrow'))
Inputs may be any that keep to these rules, and one draw needn't show every extreme that they name: `bit_orders`: each row is a permutation of 0 to 7. `phase_pairs`: qubit positions among the lowest 12; the two of a pair may coincide.
All inputs are finite; a program needn't handle non-finite values.
Results may differ from a plain program's by a relative error of at most 0.00012.
Values sent between devices are 32-bit elements; how exact they have to be, the bound alone decides.
A program may use at most 64 MiB of HBM per device.

v0:
```python
from functools import partial

import jax
import jax.numpy as jnp
from jax import lax
from jax.sharding import PartitionSpec as P

LAYERS = 6
PHASE_BITS = 12


def source_index(bit_order):
    position = jnp.arange(256, dtype=jnp.int32)
    source = jnp.zeros((256,), jnp.int32)
    for which in range(8):
        source = source + jnp.left_shift(jnp.right_shift(position, which) & 1, bit_order[which])
    return source


def complex_rows(left_re, left_im, right_re, right_im):
    product = partial(jnp.dot, preferred_element_type=jnp.float32, precision=lax.Precision.HIGHEST)
    real = product(left_re, right_re.T) - product(left_im, right_im.T)
    imag = product(left_re, right_im.T) + product(left_im, right_re.T)
    return (real, imag)


def local_gates(blocks, bit_order, matrix_re, matrix_im):
    shape_kept = blocks.shape
    flat = blocks.reshape(2, -1, 256)
    source = source_index(bit_order)
    moved = jnp.take(flat, source, axis=2)
    halves = moved.reshape(2, -1, 128)
    real, imag = complex_rows(halves[0], halves[1], matrix_re, matrix_im)
    return jnp.stack([real, imag]).reshape(shape_kept)


def apply_phase(amps, pair_row, angle_row):
    position = jnp.arange(2**PHASE_BITS, dtype=jnp.int32)
    first = jnp.right_shift(position[None, :], pair_row[:, 0:1]) & 1
    second = jnp.right_shift(position[None, :], pair_row[:, 1:2]) & 1
    phase = jnp.sum(angle_row[:, None] * (first * second).astype(jnp.float32), axis=0)
    cosine = jnp.cos(phase)
    sine = jnp.sin(phase)
    view = amps.reshape(2, -1, 2**PHASE_BITS)
    real = view[0] * cosine - view[1] * sine
    imag = view[0] * sine + view[1] * cosine
    return jnp.stack([real, imag]).reshape(amps.shape)


def one_layer(amps, matrix_re, matrix_im, bit_order, pair_row, angle_row):
    narrow_count = lax.axis_size("narrow")
    blocks = amps.reshape(2, -1, narrow_count, 256)
    swapped = lax.all_to_all(
        lax.all_to_all(blocks, "wide", split_axis=3, concat_axis=3, tiled=True),
        "narrow",
        split_axis=2,
        concat_axis=2,
        tiled=True,
    )
    gated = local_gates(swapped, bit_order, matrix_re, matrix_im)
    return apply_phase(gated.reshape(2, -1), pair_row, angle_row)


def local(state, gate_re, gate_im, bit_orders, phase_pairs, phase_angles):
    amps = state
    for layer in range(LAYERS):
        amps = one_layer(
            amps,
            gate_re[layer],
            gate_im[layer],
            bit_orders[layer],
            phase_pairs[layer],
            phase_angles[layer],
        )
    return amps


def solution(mesh):
    return jax.shard_map(
        local,
        mesh=mesh,
        in_specs=(P(None, ("wide", "narrow")), P(), P(), P(), P(), P()),
        out_specs=P(None, ("wide", "narrow")),
        check_vma=False,
    )
```

profile of v0, /device:TPU:1, one launch (start us, length us, event | category | flops | bytes accessed | tf_op | source)
XLA Modules:
  0.0 521.8 jit_solution(18314754665970048791)
XLA Ops:
  1.3 1.5 copy.178
  4.1 37.9 %all_to_all.60 = f32[32,1,8192]{2,1,0:T(1,128)S(1)} all-to-all(f32[32,1,8192]{2,1,0:T(1,128)S(1)} %reshape.1024), channel_id=1, replica_groups=mesh['wide'=32,'narrow'=8] {'wide'}, dimensions={0} | all-to-all | bytes 2097152 | tf_op jit(solution)/shard_map/all_to_all | solution.py:54
  42.5 3.2 reduce
  46.6 2.0 copy.179
  48.7 8.2 %all-to-all-start.1 = ((f32[2,64,8,256]{3,1,0,2:T(8,128)}), f32[2,64,8,256]{3,1,0,2:T(8,128)S(1)}, u32[]{:S(2)}, u32[]{:S(2)}) async-start(f32[2,64,8,256]{3,1,0,2:T(8,128)} %copy.179), calls=%async_computation.1 | async-start | bytes 2097152 | tf_op jit(solution)/shard_map/all_to_all | solution.py:53
  59.6 5.1 compare_and_fusion.5
  64.7 17.2 %all-to-all-done.1 = f32[2,64,8,256]{3,1,0,2:T(8,128)S(1)} async-done(((f32[2,64,8,256]{3,1,0,2:T(8,128)}), f32[2,64,8,256]{3,1,0,2:T(8,128)S(1)}, u32[]{:S(2)}, u32[]{:S(2)}) %all-to-all-start.1) | async-done | bytes 1048608 | tf_op jit(solution)/shard_map/all_to_all | solution.py:53
  83.1 1.8 gather_fusion
  95.4 35.3 %all_to_all.61 = f32[32,1,8192]{2,1,0:T(1,128)S(1)} all-to-all(f32[32,1,8192]{2,1,0:T(1,128)S(1)} %reshape.1026), channel_id=1, replica_groups=mesh['wide'=32,'narrow'=8] {'wide'}, dimensions={0} | all-to-all | bytes 2097152 | tf_op jit(solution)/shard_map/all_to_all | solution.py:54
  130.7 3.2 reduce.1
  134.8 2.0 copy.185
  136.8 5.0 all-to-all-start.3
  144.1 5.6 %compare_and_fusion.4 = (pred[256]{0:T(512)(128)(4,1)}, s32[256]{0:T(256)S(1)}) fusion(s32[]{:T(128)} %bitcast.39, s32[]{:T(128)} %bitcast.38, s32[]{:T(128)} %bitcast.37, s32[]{:T(128)} %bitcast.36, s32[]{:T(128)} %bitcast.35, s32[]{:T(128)} %bitcast.34, s32[]{:T(128)} %bitcast.33, s32[]{:T(128)} %bitcast.32), kind=kLoop, calls=%fused_computation.153 | loop fusion | flops 9472 | bytes 1312 | tf_op jit(solution)/shard_map/jit(_take)/and | solution.py:31
  149.7 17.3 %all-to-all-done.3 = f32[2,64,8,256]{3,1,0,2:T(8,128)S(1)} async-done(((f32[2,64,8,256]{3,1,0,2:T(8,128)}), f32[2,64,8,256]{3,1,0,2:T(8,128)S(1)}, u32[]{:S(2)}, u32[]{:S(2)}) %all-to-all-start.3) | async-done | bytes 1048608 | tf_op jit(solution)/shard_map/all_to_all | solution.py:53
  168.2 1.8 gather_fusion.1
  177.7 1.5 copy.190
  180.4 35.1 %all_to_all.62 = f32[32,1,8192]{2,1,0:T(1,128)S(1)} all-to-all(f32[32,1,8192]{2,1,0:T(1,128)S(1)} %reshape.1028), channel_id=1, replica_groups=mesh['wide'=32,'narrow'=8] {'wide'}, dimensions={0} | all-to-all | bytes 2097152 | tf_op jit(solution)/shard_map/all_to_all | solution.py:54
  215.5 3.2 reduce.2
  219.6 2.0 copy.191
  221.6 5.0 all-to-all-start.5
  228.7 5.5 %compare_and_fusion.3 = (pred[256]{0:T(512)(128)(4,1)}, s32[256]{0:T(256)S(1)}) fusion(s32[]{:T(128)} %bitcast.31, s32[]{:T(128)} %bitcast.30, s32[]{:T(128)} %bitcast.29, s32[]{:T(128)} %bitcast.28, s32[]{:T(128)} %bitcast.27, s32[]{:T(128)} %bitcast.26, s32[]{:T(128)} %bitcast.25, s32[]{:T(128)} %bitcast.24), kind=kLoop, calls=%fused_computation.152 | loop fusion | flops 9472 | bytes 1312 | tf_op jit(solution)/shard_map/jit(_take)/and | solution.py:31
  234.2 17.6 %all-to-all-done.5 = f32[2,64,8,256]{3,1,0,2:T(8,128)S(1)} async-done(((f32[2,64,8,256]{3,1,0,2:T(8,128)}), f32[2,64,8,256]{3,1,0,2:T(8,128)S(1)}, u32[]{:S(2)}, u32[]{:S(2)}) %all-to-all-start.5) | async-done | bytes 1048608 | tf_op jit(solution)/shard_map/all_to_all | solution.py:53
  253.0 1.8 gather_fusion.2
  262.4 1.5 copy.196
  265.2 35.3 %all_to_all.63 = f32[32,1,8192]{2,1,0:T(1,128)S(1)} all-to-all(f32[32,1,8192]{2,1,0:T(1,128)S(1)} %reshape.1030), channel_id=1, replica_groups=mesh['wide'=32,'narrow'=8] {'wide'}, dimensions={0} | all-to-all | bytes 2097152 | tf_op jit(solution)/shard_map/all_to_all | solution.py:54
  300.5 3.2 reduce.3
  304.6 2.0 copy.197
  306.7 5.0 all-to-all-start.7
  313.8 5.5 %compare_and_fusion.2 = (pred[256]{0:T(512)(128)(4,1)}, s32[256]{0:T(256)S(1)}) fusion(s32[]{:T(128)} %bitcast.23, s32[]{:T(128)} %bitcast.22, s32[]{:T(128)} %bitcast.21, s32[]{:T(128)} %bitcast.20, s32[]{:T(128)} %bitcast.19, s32[]{:T(128)} %bitcast.18, s32[]{:T(128)} %bitcast.17, s32[]{:T(128)} %bitcast.16), kind=kLoop, calls=%fused_computation.151 | loop fusion | flops 9472 | bytes 1312 | tf_op jit(solution)/shard_map/jit(_take)/and | solution.py:31
  319.4 17.4 %all-to-all-done.7 = f32[2,64,8,256]{3,1,0,2:T(8,128)S(1)} async-done(((f32[2,64,8,256]{3,1,0,2:T(8,128)}), f32[2,64,8,256]{3,1,0,2:T(8,128)S(1)}, u32[]{:S(2)}, u32[]{:S(2)}) %all-to-all-start.7) | async-done | bytes 1048608 | tf_op jit(solution)/shard_map/all_to_all | solution.py:53
  338.0 1.8 gather_fusion.3
  350.2 35.1 %all_to_all.64 = f32[32,1,8192]{2,1,0:T(1,128)S(1)} all-to-all(f32[32,1,8192]{2,1,0:T(1,128)S(1)} %reshape.1032), channel_id=1, replica_groups=mesh['wide'=32,'narrow'=8] {'wide'}, dimensions={0} | all-to-all | bytes 2097152 | tf_op jit(solution)/shard_map/all_to_all | solution.py:54
  385.3 3.2 reduce.4
  389.4 2.0 copy.203
  391.4 5.0 all-to-all-start.9
  397.9 5.5 %compare_and_fusion.1 = (pred[256]{0:T(512)(128)(4,1)}, s32[256]{0:T(256)S(1)}) fusion(s32[]{:T(128)} %bitcast.15, s32[]{:T(128)} %bitcast.14, s32[]{:T(128)} %bitcast.13, s32[]{:T(128)} %bitcast.12, s32[]{:T(128)} %bitcast.11, s32[]{:T(128)} %bitcast.10, s32[]{:T(128)} %bitcast.9, s32[]{:T(128)} %bitcast.8), kind=kLoop, calls=%fused_computation.150 | loop fusion | flops 9472 | bytes 1312 | tf_op jit(solution)/shard_map/jit(_take)/and | solution.py:31
  404.0 17.5 %all-to-all-done.9 = f32[2,64,8,256]{3,1,0,2:T(8,128)S(1)} async-done(((f32[2,64,8,256]{3,1,0,2:T(8,128)}), f32[2,64,8,256]{3,1,0,2:T(8,128)S(1)}, u32[]{:S(2)}, u32[]{:S(2)}) %all-to-all-start.9) | async-done | bytes 1048608 | tf_op jit(solution)/shard_map/all_to_all | solution.py:53
  422.7 1.9 gather_fusion.4
  433.8 2.3 reshape.1034
  436.1 7.6 %all-to-all-start.10 = ((f32[32,1,8192]{2,1,0:T(1,128)}), f32[32,1,8192]{2,1,0:T(1,128)S(1)}, u32[]{:S(2)}, u32[]{:S(2)}) async-start(f32[32,1,8192]{2,1,0:T(1,128)} %reshape.1034), calls=%async_computation.10 | async-start | bytes 2097152 | tf_op jit(solution)/shard_map/all_to_all | solution.py:54
  444.6 26.9 %all-to-all-done.10 = f32[32,1,8192]{2,1,0:T(1,128)S(1)} async-done(((f32[32,1,8192]{2,1,0:T(1,128)}), f32[32,1,8192]{2,1,0:T(1,128)S(1)}, u32[]{:S(2)}, u32[]{:S(2)}) %all-to-all-start.10) | async-done | bytes 1048608 | tf_op jit(solution)/shard_map/all_to_all | solution.py:54
  471.4 3.2 reduce.5
  475.5 2.0 copy.209
  477.5 5.7 %all-to-all-start.11 = ((f32[2,64,8,256]{3,1,0,2:T(8,128)}), f32[2,64,8,256]{3,1,0,2:T(8,128)S(1)}, u32[]{:S(2)}, u32[]{:S(2)}) async-start(f32[2,64,8,256]{3,1,0,2:T(8,128)} %copy.209), calls=%async_computation.11 | async-start | bytes 2097152 | tf_op jit(solution)/shard_map/all_to_all | solution.py:53
  486.0 5.0 compare_and_fusion
  491.0 17.3 %all-to-all-done.11 = f32[2,64,8,256]{3,1,0,2:T(8,128)S(1)} async-done(((f32[2,64,8,256]{3,1,0,2:T(8,128)}), f32[2,64,8,256]{3,1,0,2:T(8,128)S(1)}, u32[]{:S(2)}, u32[]{:S(2)}) %all-to-all-start.11) | async-done | bytes 1048608 | tf_op jit(solution)/shard_map/all_to_all | solution.py:53
  509.6 1.8 gather_fusion.5
  519.5 1.9 pad_maximum_fusion.5
  (221 shorter events, 85.4 us)
Async XLA Ops:
  46.6 10.3 %copy-start.12 = (s32[6,16,2]{1,2,0:T(2,128)S(1)}, s32[6,16,2]{1,2,0:T(2,128)}, u32[]{:S(2)}) copy-start(s32[6,16,2]{1,2,0:T(2,128)} %param.12) | copy-start | bytes 2308
  46.6 11.4 %copy-start.15 = (f32[6,16]{1,0:T(8,128)S(1)}, f32[6,16]{1,0:T(8,128)}, u32[]{:S(2)}) copy-start(f32[6,16]{1,0:T(8,128)} %param.13) | copy-start | bytes 1156
  46.6 12.2 %copy-start.3 = (s32[6,8]{1,0:T(8,128)S(1)}, s32[6,8]{1,0:T(8,128)}, u32[]{:S(2)}) copy-start(s32[6,8]{1,0:T(8,128)} %param.11) | copy-start | bytes 580
  48.7 33.3 %all-to-all-start.1 = ((f32[2,64,8,256]{3,1,0,2:T(8,128)}), f32[2,64,8,256]{3,1,0,2:T(8,128)S(1)}, u32[]{:S(2)}, u32[]{:S(2)}) async-start(f32[2,64,8,256]{3,1,0,2:T(8,128)} %copy.179), calls=%async_computation.1 | async-start | bytes 2097152 | tf_op jit(solution)/shard_map/all_to_all | solution.py:53
  86.8 1.1 copy-start.2
  134.8 7.1 %copy-start.24 = (f32[16]{0:T(128)S(1)}, f32[16]{0:T(128)}, u32[]{:S(2)}) copy-start(f32[16]{0:T(128)} %get-tuple-element.63) | copy-start | bytes 196
  134.8 7.1 %copy-start.25 = (s32[16]{0:T(128)S(1)}, s32[16]{0:T(128)}, u32[]{:S(2)}) copy-start(s32[16]{0:T(128)} %get-tuple-element.122) | copy-start | bytes 196
  134.8 7.1 %copy-start.26 = (s32[16]{0:T(128)S(1)}, s32[16]{0:T(128)}, u32[]{:S(2)}) copy-start(s32[16]{0:T(128)} %get-tuple-element.123) | copy-start | bytes 196
  136.8 30.1 %all-to-all-start.3 = ((f32[2,64,8,256]{3,1,0,2:T(8,128)}), f32[2,64,8,256]{3,1,0,2:T(8,128)S(1)}, u32[]{:S(2)}, u32[]{:S(2)}) async-start(f32[2,64,8,256]{3,1,0,2:T(8,128)} %copy.185), calls=%async_computation.3 | async-start | bytes 2097152 | tf_op jit(solution)/shard_map/all_to_all | solution.py:53
  168.2 1.8 copy-start.16
  176.4 0.9 copy-start.5
  176.4 1.0 copy-start.7
  219.6 7.0 %copy-start.13 = (s32[16,2]{0,1:T(2,128)S(1)}, s32[16,2]{0,1:T(2,128)}, u32[]{:S(2)}) copy-start(s32[16,2]{0,1:T(2,128)} %get-tuple-element.55) | copy-start | bytes 388
  219.6 7.0 %copy-start.14 = (s32[16,2]{0,1:T(2,128)S(1)}, s32[16,2]{0,1:T(2,128)}, u32[]{:S(2)}) copy-start(s32[16,2]{0,1:T(2,128)} %get-tuple-element.56) | copy-start | bytes 388
  219.6 7.6 %copy-start.23 = (f32[16]{0:T(128)S(1)}, f32[16]{0:T(128)}, u32[]{:S(2)}) copy-start(f32[16]{0:T(128)} %get-tuple-element.62) | copy-start | bytes 196
  221.6 30.1 %all-to-all-start.5 = ((f32[2,64,8,256]{3,1,0,2:T(8,128)}), f32[2,64,8,256]{3,1,0,2:T(8,128)S(1)}, u32[]{:S(2)}, u32[]{:S(2)}) async-start(f32[2,64,8,256]{3,1,0,2:T(8,128)} %copy.191), calls=%async_computation.5 | async-start | bytes 2097152 | tf_op jit(solution)/shard_map/all_to_all | solution.py:53
  253.0 1.8 copy-start.17
  261.2 0.9 copy-start.9
  261.2 1.0 copy-start.10
  304.6 7.0 %copy-start.22 = (f32[16]{0:T(128)S(1)}, f32[16]{0:T(128)}, u32[]{:S(2)}) copy-start(f32[16]{0:T(128)} %get-tuple-element.61) | copy-start | bytes 196
  304.6 7.0 %copy-start.27 = (s32[16]{0:T(128)S(1)}, s32[16]{0:T(128)}, u32[]{:S(2)}) copy-start(s32[16]{0:T(128)} %get-tuple-element.118) | copy-start | bytes 196
  304.6 7.0 %copy-start.28 = (s32[16]{0:T(128)S(1)}, s32[16]{0:T(128)}, u32[]{:S(2)}) copy-start(s32[16]{0:T(128)} %get-tuple-element.119) | copy-start | bytes 196
  306.7 30.1 %all-to-all-start.7 = ((f32[2,64,8,256]{3,1,0,2:T(8,128)}), f32[2,64,8,256]{3,1,0,2:T(8,128)S(1)}, u32[]{:S(2)}, u32[]{:S(2)}) async-start(f32[2,64,8,256]{3,1,0,2:T(8,128)} %copy.197), calls=%async_computation.7 | async-start | bytes 2097152 | tf_op jit(solution)/shard_map/all_to_all | solution.py:53
  337.4 2.4 copy-start.18
  346.2 0.9 copy-start.6
  346.2 1.0 copy-start.8
  389.4 7.6 %copy-start.21 = (f32[16]{0:T(128)S(1)}, f32[16]{0:T(128)}, u32[]{:S(2)}) copy-start(f32[16]{0:T(128)} %get-tuple-element.65) | copy-start | bytes 196
  391.4 30.1 %all-to-all-start.9 = ((f32[2,64,8,256]{3,1,0,2:T(8,128)}), f32[2,64,8,256]{3,1,0,2:T(8,128)S(1)}, u32[]{:S(2)}, u32[]{:S(2)}) async-start(f32[2,64,8,256]{3,1,0,2:T(8,128)} %copy.203), calls=%async_computation.9 | async-start | bytes 2097152 | tf_op jit(solution)/shard_map/all_to_all | solution.py:53
  422.7 1.9 copy-start.19
  431.1 1.0 copy-start.11
  433.8 9.9 %copy-start.20 = (f32[16]{0:T(128)S(1)}, f32[16]{0:T(128)}, u32[]{:S(2)}) copy-start(f32[16]{0:T(128)} %get-tuple-element.60) | copy-start | bytes 196
  433.8 9.9 %copy-start.29 = (s32[16]{0:T(128)S(1)}, s32[16]{0:T(128)}, u32[]{:S(2)}) copy-start(s32[16]{0:T(128)} %get-tuple-element.114) | copy-start | bytes 196
  433.8 9.9 %copy-start.30 = (s32[16]{0:T(128)S(1)}, s32[16]{0:T(128)}, u32[]{:S(2)}) copy-start(s32[16]{0:T(128)} %get-tuple-element.115) | copy-start | bytes 196
  436.1 35.3 %all-to-all-start.10 = ((f32[32,1,8192]{2,1,0:T(1,128)}), f32[32,1,8192]{2,1,0:T(1,128)S(1)}, u32[]{:S(2)}, u32[]{:S(2)}) async-start(f32[32,1,8192]{2,1,0:T(1,128)} %reshape.1034), calls=%async_computation.10 | async-start | bytes 2097152 | tf_op jit(solution)/shard_map/all_to_all | solution.py:54
  475.5 7.7 %copy-start.4 = (f32[4096]{0:T(1024)S(1)}, f32[4096]{0:T(1024)}, u32[]{:S(2)}) copy-start(f32[4096]{0:T(1024)} %get-tuple-element.43) | copy-start | bytes 49156
  477.5 30.8 %all-to-all-start.11 = ((f32[2,64,8,256]{3,1,0,2:T(8,128)}), f32[2,64,8,256]{3,1,0,2:T(8,128)S(1)}, u32[]{:S(2)}, u32[]{:S(2)}) async-start(f32[2,64,8,256]{3,1,0,2:T(8,128)} %copy.209), calls=%async_computation.11 | async-start | bytes 2097152 | tf_op jit(solution)/shard_map/all_to_all | solution.py:53
  516.3 2.1 copy-start
  516.3 2.1 copy-start.1
where the time goes:
time: 529 us; the launch traced here: 522 us
  blocking collectives  179 us (34%)
  waiting for transfers between devices  131 us (25%)
  local copies, waits for them, and re-layouts  80.7 us (15%)
  other arithmetic  63.7 us (12%)
  starting transfers between devices  41.5 us (8%)
  matrix products  24.1 us (5%)
    all_to_all x5, blocking collectives, one_layer(): lax.all_to_all(blocks, 'wide', split_axis=3, concat_axis=3, tiled=True)  179 us
    all_to_all x6, waiting for transfers between devices, one_layer(): lax.all_to_all(lax.all_to_all(blocks, 'wide', split_axis=3, concat_axis=3...  104 us
    all_to_all x6, starting transfers between devices, one_layer(): lax.all_to_all(lax.all_to_all(blocks, 'wide', split_axis=3, concat_axis=3...  33.9 us
    and x6, other arithmetic, local_gates(): moved = jnp.take(flat, source, axis=2)  32.3 us
    all_to_all x1, waiting for transfers between devices, one_layer(): lax.all_to_all(blocks, 'wide', split_axis=3, concat_axis=3, tiled=True)  26.9 us
    all_to_all x6, other arithmetic, one_layer(): lax.all_to_all(blocks, 'wide', split_axis=3, concat_axis=3, tiled=True)  19.4 us
    unnamed x79, local copies, waits for them, and re-layouts  17.9 us
    all_to_all x7, local copies, waits for them, and re-layouts, one_layer(): lax.all_to_all(blocks, 'wide', split_axis=3, concat_axis=3, tiled=True)  12.7 us
  transfers between devices with their start and end apart: 7, of which 7 were waited for; matrix products, arithmetic and copies ran while one was open for 9% of the time, Pallas kernels for 0%

commit v1 on v0

v1 whole, which is shorter than its diff:
```python
import jax
import jax.numpy as jnp
from jax import lax
from jax.experimental import pallas as pl
from jax.experimental.pallas import tpu as pltpu
from jax.sharding import PartitionSpec as P

LAYERS = 6
PHASES = 16
WIDE = 32
CHUNKS = 2
STEP_BITS = (2, 1, 3, 4, 0)


def dot_rows(left, right):
    return lax.dot_general(left, right, (((1,), (0,)), ((), ())), preferred_element_type=jnp.float32)


def split(values):
    high = values.astype(jnp.bfloat16)
    low = (values - high.astype(jnp.float32)).astype(jnp.bfloat16)
    return high, low


def transpose_granules(tiles):
    lane = lax.broadcasted_iota(jnp.int32, (8, 128), 1)
    skewed = [tiles[i] if i == 0 else pltpu.roll(tiles[i], 8 * i, 1) for i in range(16)]
    turned = [skewed[(-i) % 16] for i in range(16)]
    for bit in range(4):
        mask = (lane // (8 << bit)) % 2 == 1
        turned = [jnp.where(mask, turned[(i - (1 << bit)) % 16], turned[i]) for i in range(16)]
    return [turned[k] if k == 0 else pltpu.roll(turned[k], 128 - 8 * k, 1) for k in range(16)]


def partner(me, step):
    other = 0
    for source, target in enumerate(STEP_BITS):
        mine = (me // (1 << target)) % 2
        flip = (step // (1 << source)) % 2
        other = other + ((mine + flip) % 2) * (1 << target)
    return other


def kernel(
    bit_orders,
    phase_pairs,
    phase_angles,
    gate_re,
    gate_im,
    given,
    result,
    landed,
    leaving,
    held,
    product,
    weight_high,
    weight_low,
    cosines,
    sines,
    in_send,
    in_recv,
    out_send,
    out_recv,
    own_sem,
):
    me = lax.axis_index("wide")
    narrow = lax.axis_index("narrow")
    barrier = pltpu.get_barrier_semaphore()

    def greet(step, carry):
        pl.semaphore_signal(
            barrier, inc=1, device_id={"wide": partner(me, step)}, device_id_type=pl.DeviceIdType.MESH
        )
        return carry

    lax.fori_loop(1, WIDE, greet, 0)
    pl.semaphore_wait(barrier, WIDE - 1)

    def send_in(chunk):
        def one(step, carry):
            other = partner(me, step)
            pltpu.make_async_remote_copy(
                src_ref=given.at[other, chunk],
                dst_ref=landed.at[chunk, me],
                send_sem=in_send,
                recv_sem=in_recv.at[chunk],
                device_id={"wide": other},
                device_id_type=pl.DeviceIdType.MESH,
            ).start()
            return carry

        lax.fori_loop(1, WIDE, one, 0)

    for chunk in range(CHUNKS):
        send_in(chunk)
    for chunk in range(CHUNKS):
        pltpu.make_async_copy(given.at[me, chunk], landed.at[chunk, me], own_sem.at[chunk]).start()

    def build(layer, carry):
        gr_high, gr_low = split(gate_re[layer])
        gi_high, gi_low = split(gate_im[layer])
        lanes = lax.broadcasted_iota(jnp.int32, (128, 128), 1)
        rows = lax.broadcasted_iota(jnp.int32, (128, 128), 0)
        base = jnp.zeros((128, 128), jnp.int32)
        for which in range(7):
            base = base + jnp.left_shift(jnp.right_shift(lanes, which) & 1, bit_orders[layer, which])
        top = jnp.left_shift(jnp.int32(1), bit_orders[layer, 7])
        for h in range(2):
            for e in range(2):
                source = base + e * top
                picks = jnp.where(rows + h * 128 == source, 1.0, 0.0).astype(jnp.bfloat16)
                for store, re, im in ((weight_high, gr_high, gi_high), (weight_low, gr_low, gi_low)):
                    real = lax.dot_general(
                        picks, re, (((1,), (1,)), ((), ())), preferred_element_type=jnp.float32
                    ).astype(jnp.bfloat16)
                    imag = lax.dot_general(
                        picks, im, (((1,), (1,)), ((), ())), preferred_element_type=jnp.float32
                    ).astype(jnp.bfloat16)
                    store[layer, pl.ds(h * 256, 128), pl.ds(e * 256, 128)] = real
                    store[layer, pl.ds(h * 256, 128), pl.ds(e * 256 + 128, 128)] = imag
                    store[layer, pl.ds(h * 256 + 128, 128), pl.ds(e * 256, 128)] = -imag
                    store[layer, pl.ds(h * 256 + 128, 128), pl.ds(e * 256 + 128, 128)] = real
        return carry

    lax.fori_loop(0, LAYERS, build, 0)

    lane = lax.broadcasted_iota(jnp.int32, (8, 128), 1)
    sublane = lax.broadcasted_iota(jnp.int32, (8, 128), 0)

    def phases(layer, carry):
        odd = layer % 2
        middle = odd * sublane + (1 - odd) * narrow
        low = middle * 256 + lane
        for chunk in range(CHUNKS):
            for h in range(2):
                position = low + (chunk * 2048 + h * 128)
                phi = jnp.zeros((8, 128), jnp.float32)
                for gate in range(PHASES):
                    first = jnp.right_shift(position, phase_pairs[layer, gate, 0])
                    second = jnp.right_shift(position, phase_pairs[layer, gate, 1])
                    phi = phi + phase_angles[layer, gate] * (first & second & 1).astype(jnp.float32)
                cosines[layer, chunk, h] = jnp.cos(phi)
                sines[layer, chunk, h] = jnp.sin(phi)
        return carry

    lax.fori_loop(0, LAYERS, phases, 0)

    def one_chunk(chunk, carry):
        arrivals = landed.at[chunk, pl.ds(0, WIDE - 1)]
        pltpu.make_async_copy(arrivals, arrivals, in_recv.at[chunk]).wait()
        pltpu.make_async_copy(given.at[me, chunk], landed.at[chunk, me], own_sem.at[chunk]).wait()

        for a_high in range(2):
            for a2_high in range(2):
                for part in range(2):
                    tiles = [landed[chunk, a_high * 16 + i, a2_high * 2 + part] for i in range(16)]
                    tiles = transpose_granules(tiles)
                    for i in range(16):
                        held[a_high * 2 + part, pl.ds((a2_high * 16 + i) * 8, 8), :] = tiles[i]

        for layer in range(LAYERS):
            x = jnp.concatenate([held[k] for k in range(4)], axis=1)
            high, low = split(x)
            w_high = weight_high[layer]
            w_low = weight_low[layer]
            product[...] = dot_rows(high, w_high) + (dot_rows(low, w_high) + dot_rows(high, w_low))
            for h in range(2):
                cosine = cosines[layer, chunk, h]
                sine = sines[layer, chunk, h]
                for s in range(2):
                    reals = []
                    imags = []
                    for i in range(16):
                        rows = pl.ds((s * 16 + i) * 8, 8)
                        re = product[rows, pl.ds(h * 256, 128)]
                        im = product[rows, pl.ds(h * 256 + 128, 128)]
                        reals.append(re * cosine - im * sine)
                        imags.append(re * sine + im * cosine)
                    if layer < LAYERS - 1:
                        reals = transpose_granules(reals)
                        imags = transpose_granules(imags)
                        for i in range(16):
                            rows = pl.ds((h * 16 + i) * 8, 8)
                            held[s * 2, rows, :] = reals[i]
                            held[s * 2 + 1, rows, :] = imags[i]
                    else:
                        for i in range(16):
                            leaving[chunk, s * 16 + i, h * 2] = reals[i]
                            leaving[chunk, s * 16 + i, h * 2 + 1] = imags[i]

        def one(step, inner):
            other = partner(me, step)
            pltpu.make_async_remote_copy(
                src_ref=leaving.at[chunk, other],
                dst_ref=result.at[me, chunk],
                send_sem=out_send,
                recv_sem=out_recv,
                device_id={"wide": other},
                device_id_type=pl.DeviceIdType.MESH,
            ).start()
            return inner

        lax.fori_loop(1, WIDE, one, 0)
        pltpu.make_async_copy(leaving.at[chunk, me], result.at[me, chunk], own_sem.at[CHUNKS + chunk]).start()
        return carry

    lax.fori_loop(0, CHUNKS, one_chunk, 0)

    sent = given.at[pl.ds(0, WIDE - 1)]
    pltpu.make_async_copy(sent, sent, in_send).wait()
    for chunk in range(CHUNKS):
        pltpu.make_async_copy(leaving.at[chunk, me], result.at[me, chunk], own_sem.at[CHUNKS + chunk]).wait()
    arrived = result.at[pl.ds(0, WIDE - 1)]
    pltpu.make_async_copy(arrived, arrived, out_recv).wait()
    pltpu.make_async_copy(arrived, arrived, out_send).wait()


def run(given, bit_orders, phase_pairs, phase_angles, gate_re, gate_im):
    smem = pl.BlockSpec(memory_space=pltpu.SMEM)
    vmem = pl.BlockSpec(memory_space=pltpu.VMEM)
    return pl.pallas_call(
        kernel,
        out_shape=jax.ShapeDtypeStruct((WIDE, CHUNKS, 4, 8, 128), jnp.float32),
        in_specs=[smem, smem, smem, vmem, vmem, vmem],
        out_specs=vmem,
        scratch_shapes=[
            pltpu.VMEM((CHUNKS, WIDE, 4, 8, 128), jnp.float32),
            pltpu.VMEM((CHUNKS, WIDE, 4, 8, 128), jnp.float32),
            pltpu.VMEM((4, 256, 128), jnp.float32),
            pltpu.VMEM((256, 512), jnp.float32),
            pltpu.VMEM((LAYERS, 512, 512), jnp.bfloat16),
            pltpu.VMEM((LAYERS, 512, 512), jnp.bfloat16),
            pltpu.VMEM((LAYERS, CHUNKS, 2, 8, 128), jnp.float32),
            pltpu.VMEM((LAYERS, CHUNKS, 2, 8, 128), jnp.float32),
            pltpu.SemaphoreType.DMA,
            pltpu.SemaphoreType.DMA((CHUNKS,)),
            pltpu.SemaphoreType.DMA,
            pltpu.SemaphoreType.DMA,
            pltpu.SemaphoreType.DMA((2 * CHUNKS,)),
        ],
        compiler_params=pltpu.CompilerParams(
            collective_id=0, has_side_effects=True, vmem_limit_bytes=32 * 1024 * 1024
        ),
        cost_estimate=pl.CostEstimate(flops=4_831_838_208, bytes_accessed=4_194_304, transcendentals=49_152),
    )(bit_orders, phase_pairs, phase_angles, gate_re, gate_im, given)


def local(state, gate_re, gate_im, bit_orders, phase_pairs, phase_angles):
    view = state.reshape(2, WIDE, CHUNKS, 8, 2, 128)
    given = view.transpose(1, 2, 4, 0, 3, 5).reshape(WIDE, CHUNKS, 4, 8, 128)
    result = run(given, bit_orders, phase_pairs, phase_angles, gate_re, gate_im)
    back = result.reshape(WIDE, CHUNKS, 2, 2, 8, 128).transpose(3, 0, 1, 4, 2, 5)
    return back.reshape(state.shape)


def solution(mesh):
    return jax.shard_map(
        local,
        mesh=mesh,
        in_specs=(P(None, ("wide", "narrow")), P(), P(), P(), P(), P()),
        out_specs=P(None, ("wide", "narrow")),
        check_vma=False,
    )
```

time: 529 us -> 66.8 us (0.13); the launches traced: 522 us -> 66.7 us
  blocking collectives: 179 us -> 0 us
  waiting for transfers between devices: 131 us -> 0 us
  local copies, waits for them, and re-layouts: 80.7 us -> 7.09 us
  other arithmetic: 63.7 us -> 0 us
  Pallas kernels: 0 us -> 59.5 us
  starting transfers between devices: 41.5 us -> 0 us
  matrix products: 24.1 us -> 0 us
    all_to_all x5 -> x0, blocking collectives: 179 us -> none  [one_layer(): lax.all_to_all(blocks, 'wide', split_axis=3, concat_axis=3, tiled=True)]
    all_to_all x7 -> x0, waiting for transfers between devices: 131 us -> none  [the longest x6 104 us: one_layer(): lax.all_to_all(lax.all_to_all(blocks, 'wide', split_axis=3, concat_axis=3...]
    pallas_call x0 -> x1, Pallas kernels: none -> 59.5 us  [run(): pl.pallas_call(kernel, out_shape=jax.ShapeDtypeStruct((WIDE, CHUNKS, 4, 8...]
    all_to_all x7 -> x0, starting transfers between devices: 41.5 us -> none  [the longest x6 33.9 us: one_layer(): lax.all_to_all(lax.all_to_all(blocks, 'wide', split_axis=3, concat_axis=3...]
    and x6 -> x0, other arithmetic: 32.3 us -> none  [local_gates(): moved = jnp.take(flat, source, axis=2)]
    dot_general x24 -> x0, matrix products: 24.1 us -> none  [the longest x12 12 us: complex_rows(): real = product(left_re, right_re.T) - product(left_im, right_im.T)]
    all_to_all x6 -> x0, other arithmetic: 19.4 us -> none  [one_layer(): lax.all_to_all(blocks, 'wide', split_axis=3, concat_axis=3, tiled=True)]
    all_to_all x13 -> x0, local copies, waits for them, and re-layouts: 16.3 us -> none  [the longest x7 12.7 us: one_layer(): lax.all_to_all(blocks, 'wide', split_axis=3, concat_axis=3, tiled=True)]
  transfers between devices with their start and end apart: 7 -> 0, of which waited for: 7 -> 0; matrix products, arithmetic and copies ran while one was open for 9% -> 0% of each run, Pallas kernels for 0% -> 0%
where the time goes in v1:
time: 66.8 us; the launch traced here: 66.7 us
  Pallas kernels  59.5 us (89%)
  local copies, waits for them, and re-layouts  7.09 us (11%)
    pallas_call x1, Pallas kernels, run(): pl.pallas_call(kernel, out_shape=jax.ShapeDtypeStruct((WIDE, CHUNKS, 4, 8...  59.5 us
    reshape x2, local copies, waits for them, and re-layouts, local(): view = state.reshape(2, WIDE, CHUNKS, 8, 2, 128)  2.62 us
    reshape x1, local copies, waits for them, and re-layouts, local(): return back.reshape(state.shape)  2.17 us
    unnamed x9, local copies, waits for them, and re-layouts  1.74 us

profile of v1, /device:TPU:1, one launch (start us, length us, event | category | flops | bytes accessed | tf_op | source)
XLA Modules:
  0.0 66.7 jit_solution(15183218089514306037)
XLA Ops:
  0.0 0.8 %copy.8.phase_pairs = s32[6,16,2]{2,1,0:T(8,128)S(1)} copy(s32[6,16,2]{1,2,0:T(2,128)} %param.10) | data formatting | bytes 1536 | tf_op args[4]
  0.8 2.5 %reshape.12 = f32[2,32,2,8,2,128]{5,4,3,2,1,0:T(2,128)S(1)} reshape(f32[2,131072]{1,0:T(2,128)} %param.6) | data formatting | bytes 2097152 | tf_op jit(solution)/shard_map/reshape | solution.py:249
  3.3 0.0 copy-start
  3.3 0.0 copy-start.1
  3.3 0.0 copy-start.2
  3.3 0.0 copy-start.3
  3.3 0.1 copy.7
  3.5 0.8 %copy-done = f32[6,128,128]{2,1,0:T(8,128)S(1)} copy-done((f32[6,128,128]{2,1,0:T(8,128)S(1)}, f32[6,128,128]{2,1,0:T(8,128)}, u32[]{:S(2)}) %copy-start) | copy-done | bytes 393240
  4.3 0.1 copy-done.1
  4.4 0.0 copy-done.2
  4.4 0.0 copy-done.3
  4.4 59.5 %shard_map.64 = f32[32,2,4,8,128]{4,3,2,1,0:T(8,128)S(1)} custom-call(s32[6,8]{1,0:T(8,128)S(1)} %copy-done.2, s32[6,16,2]{2,1,0:T(8,128)S(1)} %copy.8.phase_pairs, f32[6,16]{1,0:T(8,128)S(1)} %copy-done.3, f32[6,128,128]{2,1,0:T(8,128)S(1)} %copy-done, f32[6,128,128]{2,1,0:T(8,128)S(1)} %copy-done.1, f32[32,2,4,8,128]{4,3,2,1,0:T(8,128)S(1)} %bitcast.6), custom_call_target="tpu_custom_call" | custom-call | flops 4831838208 | bytes 4194304 | tf_op jit(solution)/shard_map/pallas_call | solution.py:221
  63.9 0.6 copy.9
  64.5 2.2 %reshape.15 = f32[2,131072]{1,0:T(2,128)} reshape(f32[2,32,2,8,2,128]{5,4,3,2,1,0:T(2,128)S(1)} %copy.9) | data formatting | bytes 2097152 | tf_op jit(solution)/shard_map/reshape | solution.py:253
Async XLA Ops:
  3.3 1.0 %copy-start = (f32[6,128,128]{2,1,0:T(8,128)S(1)}, f32[6,128,128]{2,1,0:T(8,128)}, u32[]{:S(2)}) copy-start(f32[6,128,128]{2,1,0:T(8,128)} %gate_re.1) | copy-start | bytes 1179652
  3.3 1.1 %copy-start.1 = (f32[6,128,128]{2,1,0:T(8,128)S(1)}, f32[6,128,128]{2,1,0:T(8,128)}, u32[]{:S(2)}) copy-start(f32[6,128,128]{2,1,0:T(8,128)} %gate_im.1) | copy-start | bytes 1179652
  3.3 1.1 %copy-start.2 = (s32[6,8]{1,0:T(8,128)S(1)}, s32[6,8]{1,0:T(8,128)}, u32[]{:S(2)}) copy-start(s32[6,8]{1,0:T(8,128)} %bit_orders.1) | copy-start | bytes 580
  3.3 1.1 %copy-start.3 = (f32[6,16]{1,0:T(8,128)S(1)}, f32[6,16]{1,0:T(8,128)}, u32[]{:S(2)}) copy-start(f32[6,16]{1,0:T(8,128)} %phase_angles.1) | copy-start | bytes 1156

commit v2 on v1

--- a/solution.py
+++ b/solution.py
@@ -9,7 +9,9 @@
 PHASES = 16
 WIDE = 32
 CHUNKS = 2
-STEP_BITS = (2, 1, 3, 4, 0)
+NEAR = [k for k in range(1, 32) if not k & 4]
+FAR = [k for k in range(1, 32) if k & 4]
+ORDERS = (list(range(1, 32)),) * 4
 
 
 def dot_rows(left, right):
@@ -32,23 +34,24 @@
     return [turned[k] if k == 0 else pltpu.roll(turned[k], 128 - 8 * k, 1) for k in range(16)]
 
 
-def partner(me, step):
-    other = 0
-    for source, target in enumerate(STEP_BITS):
-        mine = (me // (1 << target)) % 2
-        flip = (step // (1 << source)) % 2
-        other = other + ((mine + flip) % 2) * (1 << target)
-    return other
+def partners(me):
+    turns = [(1 - 2 * ((me // (1 << bit)) % 2)) * (1 << bit) for bit in range(5)]
+    return [me + sum(turns[bit] for bit in range(5) if (distance >> bit) & 1) for distance in range(WIDE)]
 
 
 def kernel(
+    given,
+    gate_re_given,
+    gate_im_given,
+    bit_orders_given,
+    phase_pairs_given,
+    phase_angles_given,
+    result,
+    gate_re,
+    gate_im,
     bit_orders,
     phase_pairs,
     phase_angles,
-    gate_re,
-    gate_im,
-    given,
-    result,
     landed,
     leaving,
     held,
@@ -62,39 +65,48 @@
     out_send,
     out_recv,
     own_sem,
+    fetch_sem,
 ):
     me = lax.axis_index("wide")
     narrow = lax.axis_index("narrow")
     barrier = pltpu.get_barrier_semaphore()
 
-    def greet(step, carry):
+    others = partners(me)
+    for distance in range(1, WIDE):
         pl.semaphore_signal(
-            barrier, inc=1, device_id={"wide": partner(me, step)}, device_id_type=pl.DeviceIdType.MESH
+            barrier, inc=1, device_id={"wide": others[distance]}, device_id_type=pl.DeviceIdType.MESH
         )
-        return carry
-
-    lax.fori_loop(1, WIDE, greet, 0)
+    parameters = [
+        pltpu.make_async_copy(source, target, fetch_sem.at[i])
+        for i, (source, target) in enumerate(
+            [
+                (gate_re_given, gate_re),
+                (gate_im_given, gate_im),
+                (bit_orders_given, bit_orders),
+                (phase_pairs_given, phase_pairs),
+                (phase_angles_given, phase_angles),
+            ]
+        )
+    ]
+    for copy in parameters:
+        copy.start()
     pl.semaphore_wait(barrier, WIDE - 1)
 
-    def send_in(chunk):
-        def one(step, carry):
-            other = partner(me, step)
+    for chunk in range(CHUNKS):
+        for distance in ORDERS[chunk]:
             pltpu.make_async_remote_copy(
-                src_ref=given.at[other, chunk],
+                src_ref=given.at[others[distance], chunk],
                 dst_ref=landed.at[chunk, me],
                 send_sem=in_send,
                 recv_sem=in_recv.at[chunk],
-                device_id={"wide": other},
+                device_id={"wide": others[distance]},
                 device_id_type=pl.DeviceIdType.MESH,
             ).start()
-            return carry
-
-        lax.fori_loop(1, WIDE, one, 0)
-
-    for chunk in range(CHUNKS):
-        send_in(chunk)
     for chunk in range(CHUNKS):
         pltpu.make_async_copy(given.at[me, chunk], landed.at[chunk, me], own_sem.at[chunk]).start()
+
+    for copy in parameters:
+        copy.wait()
 
     def build(layer, carry):
         gr_high, gr_low = split(gate_re[layer])
@@ -136,8 +148,8 @@
                 position = low + (chunk * 2048 + h * 128)
                 phi = jnp.zeros((8, 128), jnp.float32)
                 for gate in range(PHASES):
-                    first = jnp.right_shift(position, phase_pairs[layer, gate, 0])
-                    second = jnp.right_shift(position, phase_pairs[layer, gate, 1])
+                    first = jnp.right_shift(position, phase_pairs[layer, 0, gate])
+                    second = jnp.right_shift(position, phase_pairs[layer, 1, gate])
                     phi = phi + phase_angles[layer, gate] * (first & second & 1).astype(jnp.float32)
                 cosines[layer, chunk, h] = jnp.cos(phi)
                 sines[layer, chunk, h] = jnp.sin(phi)
@@ -153,7 +165,8 @@
         for a_high in range(2):
             for a2_high in range(2):
                 for part in range(2):
-                    tiles = [landed[chunk, a_high * 16 + i, a2_high * 2 + part] for i in range(16)]
+                    rows = pl.ds(a2_high * 2 + part, 8, stride=4)
+                    tiles = [landed[chunk, a_high * 16 + i, rows, :] for i in range(16)]
                     tiles = transpose_granules(tiles)
                     for i in range(16):
                         held[a_high * 2 + part, pl.ds((a2_high * 16 + i) * 8, 8), :] = tiles[i]
@@ -185,22 +198,18 @@
                             held[s * 2 + 1, rows, :] = imags[i]
                     else:
                         for i in range(16):
-                            leaving[chunk, s * 16 + i, h * 2] = reals[i]
-                            leaving[chunk, s * 16 + i, h * 2 + 1] = imags[i]
-
-        def one(step, inner):
-            other = partner(me, step)
+                            leaving[chunk, s * 16 + i, pl.ds(h * 2, 8, stride=4), :] = reals[i]
+                            leaving[chunk, s * 16 + i, pl.ds(h * 2 + 1, 8, stride=4), :] = imags[i]
+
+        for distance in ORDERS[2]:
             pltpu.make_async_remote_copy(
-                src_ref=leaving.at[chunk, other],
+                src_ref=leaving.at[chunk, others[distance]],
                 dst_ref=result.at[me, chunk],
                 send_sem=out_send,
                 recv_sem=out_recv,
-                device_id={"wide": other},
+                device_id={"wide": others[distance]},
                 device_id_type=pl.DeviceIdType.MESH,
             ).start()
-            return inner
-
-        lax.fori_loop(1, WIDE, one, 0)
         pltpu.make_async_copy(leaving.at[chunk, me], result.at[me, chunk], own_sem.at[CHUNKS + chunk]).start()
         return carry
 
@@ -215,17 +224,21 @@
     pltpu.make_async_copy(arrived, arrived, out_send).wait()
 
 
-def run(given, bit_orders, phase_pairs, phase_angles, gate_re, gate_im):
-    smem = pl.BlockSpec(memory_space=pltpu.SMEM)
-    vmem = pl.BlockSpec(memory_space=pltpu.VMEM)
+def run(given, gate_re, gate_im, bit_orders, phase_pairs, phase_angles):
+    operands = (given, gate_re, gate_im, bit_orders, phase_pairs, phase_angles)
     return pl.pallas_call(
         kernel,
-        out_shape=jax.ShapeDtypeStruct((WIDE, CHUNKS, 4, 8, 128), jnp.float32),
-        in_specs=[smem, smem, smem, vmem, vmem, vmem],
-        out_specs=vmem,
+        out_shape=pltpu.VMEM(given.shape, jnp.float32),
+        in_specs=[pl.BlockSpec(memory_space=pltpu.HBM)] * len(operands),
+        out_specs=pl.BlockSpec(memory_space=pltpu.VMEM),
         scratch_shapes=[
-            pltpu.VMEM((CHUNKS, WIDE, 4, 8, 128), jnp.float32),
-            pltpu.VMEM((CHUNKS, WIDE, 4, 8, 128), jnp.float32),
+            pltpu.VMEM(gate_re.shape, jnp.float32),
+            pltpu.VMEM(gate_im.shape, jnp.float32),
+            pltpu.SMEM(bit_orders.shape, jnp.int32),
+            pltpu.SMEM(phase_pairs.shape, jnp.int32),
+            pltpu.SMEM(phase_angles.shape, jnp.float32),
+            pltpu.VMEM((CHUNKS, WIDE, 32, 128), jnp.float32),
+            pltpu.VMEM((CHUNKS, WIDE, 32, 128), jnp.float32),
             pltpu.VMEM((4, 256, 128), jnp.float32),
             pltpu.VMEM((256, 512), jnp.float32),
             pltpu.VMEM((LAYERS, 512, 512), jnp.bfloat16),
@@ -237,20 +250,19 @@
             pltpu.SemaphoreType.DMA,
             pltpu.SemaphoreType.DMA,
             pltpu.SemaphoreType.DMA((2 * CHUNKS,)),
+            pltpu.SemaphoreType.DMA((5,)),
         ],
         compiler_params=pltpu.CompilerParams(
-            collective_id=0, has_side_effects=True, vmem_limit_bytes=32 * 1024 * 1024
+            collective_id=0, has_side_effects=True, vmem_limit_bytes=48 * 1024 * 1024
         ),
         cost_estimate=pl.CostEstimate(flops=4_831_838_208, bytes_accessed=4_194_304, transcendentals=49_152),
-    )(bit_orders, phase_pairs, phase_angles, gate_re, gate_im, given)
+    )(*[pltpu.with_memory_space_constraint(x, pltpu.HBM) for x in operands])
 
 
 def local(state, gate_re, gate_im, bit_orders, phase_pairs, phase_angles):
-    view = state.reshape(2, WIDE, CHUNKS, 8, 2, 128)
-    given = view.transpose(1, 2, 4, 0, 3, 5).reshape(WIDE, CHUNKS, 4, 8, 128)
-    result = run(given, bit_orders, phase_pairs, phase_angles, gate_re, gate_im)
-    back = result.reshape(WIDE, CHUNKS, 2, 2, 8, 128).transpose(3, 0, 1, 4, 2, 5)
-    return back.reshape(state.shape)
+    given = state.reshape(2, 1024, 128).transpose(1, 0, 2).reshape(WIDE, CHUNKS, 32, 128)
+    result = run(given, gate_re, gate_im, bit_orders, phase_pairs.transpose(0, 2, 1), phase_angles)
+    return result.reshape(1024, 2, 128).transpose(1, 0, 2).reshape(state.shape)
 
 
 def solution(mesh):

time: 66.8 us -> 56.9 us (0.85)
  local copies, waits for them, and re-layouts: 7.09 us -> 0.97 us
  Pallas kernels: 59.5 us -> 55.9 us
    reshape x3 -> x0, local copies, waits for them, and re-layouts: 4.79 us -> none  [the longest x2 2.62 us: local(): view = state.reshape(2, WIDE, CHUNKS, 8, 2, 128)]
    pallas_call x1, Pallas kernels: 59.5 us -> 55.9 us  [run(): pl.pallas_call(kernel, out_shape=pltpu.VMEM(given.shape, jnp.float32), in...]
    unnamed x9 -> x1, local copies, waits for them, and re-layouts: 1.74 us -> 0.97 us
where the time goes in v2:
time: 56.9 us; the launch traced here: 56.8 us
  Pallas kernels  55.9 us (98%)
  local copies, waits for them, and re-layouts  0.97 us (2%)
    pallas_call x1, Pallas kernels, run(): pl.pallas_call(kernel, out_shape=pltpu.VMEM(given.shape, jnp.float32), in...  55.9 us

profile of v2, /device:TPU:1, one launch (start us, length us, event | category | flops | bytes accessed | tf_op | source)
XLA Modules:
  0.0 56.8 jit_solution(7503940328671396006)
XLA Ops:
  0.0 55.9 %shard_map.64 = f32[32,2,32,128]{3,2,1,0:T(8,128)S(1)} custom-call(f32[32,2,32,128]{3,2,1,0:T(8,128)} %bitcast.12, f32[6,128,128]{2,1,0:T(8,128)} %gate_re_given.1, f32[6,128,128]{2,1,0:T(8,128)} %gate_im_given.1, s32[6,8]{1,0:T(8,128)} %bit_orders_given.1, s32[6,2,16]{2,1,0:T(2,128)} %bitcast.13, f32[6,16]{1,0:T(8,128)} %phase_angles_given.1), custom_call_target="tpu_custom_call" | custom-call | flops 4831838208 | bytes 4194304 | tf_op jit(solution)/shard_map/pallas_call | solution.py:229
  55.9 1.0 %copy.10 = f32[2,131072]{1,0:T(2,128)} copy(f32[2,131072]{1,0:T(2,128)S(1)} %bitcast.11) | data formatting | bytes 2097152

commit v3 on v2

--- a/solution.py
+++ b/solution.py
@@ -9,9 +9,6 @@
 PHASES = 16
 WIDE = 32
 CHUNKS = 2
-NEAR = [k for k in range(1, 32) if not k & 4]
-FAR = [k for k in range(1, 32) if k & 4]
-ORDERS = (list(range(1, 32)),) * 4
 
 
 def dot_rows(left, right):
@@ -40,7 +37,7 @@
 
 
 def kernel(
-    given,
+    given_there,
     gate_re_given,
     gate_im_given,
     bit_orders_given,
@@ -66,13 +63,17 @@
     out_recv,
     own_sem,
     fetch_sem,
+    given,
 ):
     me = lax.axis_index("wide")
     narrow = lax.axis_index("narrow")
     barrier = pltpu.get_barrier_semaphore()
 
     others = partners(me)
-    for distance in range(1, WIDE):
+    swing = (me // 2) % 2
+    turned = partners(me + swing * 4 * (1 - 2 * ((me // 4) % 2)))
+    sequence = [turned[i] for i in range(WIDE - 1, 0, -1) if i != 4] + [others[4]]
+    for distance in range(WIDE - 1, 0, -1):
         pl.semaphore_signal(
             barrier, inc=1, device_id={"wide": others[distance]}, device_id_type=pl.DeviceIdType.MESH
         )
@@ -85,27 +86,29 @@
                 (bit_orders_given, bit_orders),
                 (phase_pairs_given, phase_pairs),
                 (phase_angles_given, phase_angles),
+                (given_there, given),
             ]
         )
     ]
-    for copy in parameters:
+    for copy in parameters[::-1]:
         copy.start()
+    parameters[5].wait()
     pl.semaphore_wait(barrier, WIDE - 1)
 
     for chunk in range(CHUNKS):
-        for distance in ORDERS[chunk]:
+        for other in sequence:
             pltpu.make_async_remote_copy(
-                src_ref=given.at[others[distance], chunk],
+                src_ref=given.at[other, chunk],
                 dst_ref=landed.at[chunk, me],
                 send_sem=in_send,
                 recv_sem=in_recv.at[chunk],
-                device_id={"wide": others[distance]},
+                device_id={"wide": other},
                 device_id_type=pl.DeviceIdType.MESH,
             ).start()
     for chunk in range(CHUNKS):
         pltpu.make_async_copy(given.at[me, chunk], landed.at[chunk, me], own_sem.at[chunk]).start()
 
-    for copy in parameters:
+    for copy in parameters[:5]:
         copy.wait()
 
     def build(layer, carry):
@@ -201,13 +204,13 @@
                             leaving[chunk, s * 16 + i, pl.ds(h * 2, 8, stride=4), :] = reals[i]
                             leaving[chunk, s * 16 + i, pl.ds(h * 2 + 1, 8, stride=4), :] = imags[i]
 
-        for distance in ORDERS[2]:
+        for other in sequence:
             pltpu.make_async_remote_copy(
-                src_ref=leaving.at[chunk, others[distance]],
+                src_ref=leaving.at[chunk, other],
                 dst_ref=result.at[me, chunk],
                 send_sem=out_send,
                 recv_sem=out_recv,
-                device_id={"wide": others[distance]},
+                device_id={"wide": other},
                 device_id_type=pl.DeviceIdType.MESH,
             ).start()
         pltpu.make_async_copy(leaving.at[chunk, me], result.at[me, chunk], own_sem.at[CHUNKS + chunk]).start()
@@ -250,7 +253,8 @@
             pltpu.SemaphoreType.DMA,
             pltpu.SemaphoreType.DMA,
             pltpu.SemaphoreType.DMA((2 * CHUNKS,)),
-            pltpu.SemaphoreType.DMA((5,)),
+            pltpu.SemaphoreType.DMA((6,)),
+            pltpu.VMEM(given.shape, jnp.float32),
         ],
         compiler_params=pltpu.CompilerParams(
             collective_id=0, has_side_effects=True, vmem_limit_bytes=48 * 1024 * 1024

time: 56.9 us -> 55.6 us (0.977)
  Pallas kernels: 55.9 us -> 54.5 us
    pallas_call x1, Pallas kernels: 55.9 us -> 54.5 us  [run(): pl.pallas_call(kernel, out_shape=pltpu.VMEM(given.shape, jnp.float32), in...]
where the time goes in v3:
time: 55.6 us; the launch traced here: 55.5 us
  Pallas kernels  54.5 us (98%)
  local copies, waits for them, and re-layouts  0.97 us (2%)
    pallas_call x1, Pallas kernels, run(): pl.pallas_call(kernel, out_shape=pltpu.VMEM(given.shape, jnp.float32), in...  54.5 us

profile of v3, /device:TPU:1, one launch (start us, length us, event | category | flops | bytes accessed | tf_op | source)
XLA Modules:
  0.0 55.5 jit_solution(15125356505337986767)
XLA Ops:
  0.0 54.5 %shard_map.64 = f32[32,2,32,128]{3,2,1,0:T(8,128)S(1)} custom-call(f32[32,2,32,128]{3,2,1,0:T(8,128)} %bitcast.12, f32[6,128,128]{2,1,0:T(8,128)} %gate_re_given.1, f32[6,128,128]{2,1,0:T(8,128)} %gate_im_given.1, s32[6,8]{1,0:T(8,128)} %bit_orders_given.1, s32[6,2,16]{2,1,0:T(2,128)} %bitcast.13, f32[6,16]{1,0:T(8,128)} %phase_angles_given.1), custom_call_target="tpu_custom_call" | custom-call | flops 4831838208 | bytes 4194304 | tf_op jit(solution)/shard_map/pallas_call | solution.py:232
  54.5 1.0 %copy.10 = f32[2,131072]{1,0:T(2,128)} copy(f32[2,131072]{1,0:T(2,128)S(1)} %bitcast.11) | data formatting | bytes 2097152

commit v4 on v3

--- a/solution.py
+++ b/solution.py
@@ -37,7 +37,7 @@
 
 
 def kernel(
-    given_there,
+    given,
     gate_re_given,
     gate_im_given,
     bit_orders_given,
@@ -63,7 +63,7 @@
     out_recv,
     own_sem,
     fetch_sem,
-    given,
+    lines,
 ):
     me = lax.axis_index("wide")
     narrow = lax.axis_index("narrow")
@@ -73,7 +73,7 @@
     swing = (me // 2) % 2
     turned = partners(me + swing * 4 * (1 - 2 * ((me // 4) % 2)))
     sequence = [turned[i] for i in range(WIDE - 1, 0, -1) if i != 4] + [others[4]]
-    for distance in range(WIDE - 1, 0, -1):
+    for distance in (24, 16, 8, 7, 6, 5, 4, 3, 2, 1):
         pl.semaphore_signal(
             barrier, inc=1, device_id={"wide": others[distance]}, device_id_type=pl.DeviceIdType.MESH
         )
@@ -86,17 +86,17 @@
                 (bit_orders_given, bit_orders),
                 (phase_pairs_given, phase_pairs),
                 (phase_angles_given, phase_angles),
-                (given_there, given),
             ]
         )
     ]
-    for copy in parameters[::-1]:
-        copy.start()
-    parameters[5].wait()
-    pl.semaphore_wait(barrier, WIDE - 1)
-
-    for chunk in range(CHUNKS):
-        for other in sequence:
+    pl.semaphore_wait(barrier, 10)
+    for distance in (24, 16, 8):
+        pl.semaphore_signal(
+            lines, inc=1, device_id={"wide": others[distance]}, device_id_type=pl.DeviceIdType.MESH
+        )
+
+    def send_in(chunk, targets):
+        for other in targets:
             pltpu.make_async_remote_copy(
                 src_ref=given.at[other, chunk],
                 dst_ref=landed.at[chunk, me],
@@ -105,10 +105,17 @@
                 device_id={"wide": other},
                 device_id_type=pl.DeviceIdType.MESH,
             ).start()
+
+    send_in(0, sequence[24:])
+    pl.semaphore_wait(lines, 3)
+    send_in(0, sequence[:24])
+    send_in(1, sequence)
     for chunk in range(CHUNKS):
         pltpu.make_async_copy(given.at[me, chunk], landed.at[chunk, me], own_sem.at[chunk]).start()
 
-    for copy in parameters[:5]:
+    for copy in parameters:
+        copy.start()
+    for copy in parameters:
         copy.wait()
 
     def build(layer, carry):
@@ -253,8 +260,8 @@
             pltpu.SemaphoreType.DMA,
             pltpu.SemaphoreType.DMA,
             pltpu.SemaphoreType.DMA((2 * CHUNKS,)),
-            pltpu.SemaphoreType.DMA((6,)),
-            pltpu.VMEM(given.shape, jnp.float32),
+            pltpu.SemaphoreType.DMA((5,)),
+            pltpu.SemaphoreType.REGULAR,
         ],
         compiler_params=pltpu.CompilerParams(
             collective_id=0, has_side_effects=True, vmem_limit_bytes=48 * 1024 * 1024

time: 55.6 us -> 54.3 us (0.977)
  Pallas kernels: 54.5 us -> 53.2 us
    pallas_call x1, Pallas kernels: 54.5 us -> 53.2 us  [run(): pl.pallas_call(kernel, out_shape=pltpu.VMEM(given.shape, jnp.float32), in...]
where the time goes in v4:
time: 54.3 us; the launch traced here: 54.2 us
  Pallas kernels  53.2 us (98%)
  local copies, waits for them, and re-layouts  0.97 us (2%)
    pallas_call x1, Pallas kernels, run(): pl.pallas_call(kernel, out_shape=pltpu.VMEM(given.shape, jnp.float32), in...  53.2 us

profile of v4, /device:TPU:1, one launch (start us, length us, event | category | flops | bytes accessed | tf_op | source)
XLA Modules:
  0.0 54.2 jit_solution(3928470334810104089)
XLA Ops:
  0.0 53.2 %shard_map.64 = f32[32,2,32,128]{3,2,1,0:T(8,128)S(1)} custom-call(f32[32,2,32,128]{3,2,1,0:T(8,128)} %bitcast.12, f32[6,128,128]{2,1,0:T(8,128)} %gate_re_given.1, f32[6,128,128]{2,1,0:T(8,128)} %gate_im_given.1, s32[6,8]{1,0:T(8,128)} %bit_orders_given.1, s32[6,2,16]{2,1,0:T(2,128)} %bitcast.13, f32[6,16]{1,0:T(8,128)} %phase_angles_given.1), custom_call_target="tpu_custom_call" | custom-call | flops 4831838208 | bytes 4194304 | tf_op jit(solution)/shard_map/pallas_call | solution.py:239
  53.2 1.0 %copy.10 = f32[2,131072]{1,0:T(2,128)} copy(f32[2,131072]{1,0:T(2,128)S(1)} %bitcast.11) | data formatting | bytes 2097152

commit v5 on v4

--- a/solution.py
+++ b/solution.py
@@ -90,9 +90,9 @@
         )
     ]
     pl.semaphore_wait(barrier, 10)
-    for distance in (24, 16, 8):
+    for line, distance in enumerate((8, 16, 24)):
         pl.semaphore_signal(
-            lines, inc=1, device_id={"wide": others[distance]}, device_id_type=pl.DeviceIdType.MESH
+            lines.at[line], inc=1, device_id={"wide": others[distance]}, device_id_type=pl.DeviceIdType.MESH
         )
 
     def send_in(chunk, targets):
@@ -107,9 +107,10 @@
             ).start()
 
     send_in(0, sequence[24:])
-    pl.semaphore_wait(lines, 3)
-    send_in(0, sequence[:24])
-    send_in(1, sequence)
+    for line in range(3):
+        pl.semaphore_wait(lines.at[line], 1)
+        send_in(0, sequence[16 - 8 * line : 24 - 8 * line])
+    send_in(1, sequence[:8] + sequence[24:] + sequence[8:24])
     for chunk in range(CHUNKS):
         pltpu.make_async_copy(given.at[me, chunk], landed.at[chunk, me], own_sem.at[chunk]).start()
 
@@ -261,7 +262,7 @@
             pltpu.SemaphoreType.DMA,
             pltpu.SemaphoreType.DMA((2 * CHUNKS,)),
             pltpu.SemaphoreType.DMA((5,)),
-            pltpu.SemaphoreType.REGULAR,
+            pltpu.SemaphoreType.REGULAR((3,)),
         ],
         compiler_params=pltpu.CompilerParams(
             collective_id=0, has_side_effects=True, vmem_limit_bytes=48 * 1024 * 1024

time: 54.3 us -> 54.1 us (level)
  no operation moved by 1% of the time
where the time goes in v5:
time: 54.1 us; the launch traced here: 54 us
  Pallas kernels  53.1 us (98%)
  local copies, waits for them, and re-layouts  0.97 us (2%)
    pallas_call x1, Pallas kernels, run(): pl.pallas_call(kernel, out_shape=pltpu.VMEM(given.shape, jnp.float32), in...  53.1 us

profile of v5, /device:TPU:1, one launch (start us, length us, event | category | flops | bytes accessed | tf_op | source)
XLA Modules:
  0.0 54.0 jit_solution(16374225750451431907)
XLA Ops:
  0.0 53.1 %shard_map.64 = f32[32,2,32,128]{3,2,1,0:T(8,128)S(1)} custom-call(f32[32,2,32,128]{3,2,1,0:T(8,128)} %bitcast.12, f32[6,128,128]{2,1,0:T(8,128)} %gate_re_given.1, f32[6,128,128]{2,1,0:T(8,128)} %gate_im_given.1, s32[6,8]{1,0:T(8,128)} %bit_orders_given.1, s32[6,2,16]{2,1,0:T(2,128)} %bitcast.13, f32[6,16]{1,0:T(8,128)} %phase_angles_given.1), custom_call_target="tpu_custom_call" | custom-call | flops 4831838208 | bytes 4194304 | tf_op jit(solution)/shard_map/pallas_call | solution.py:240
  53.1 1.0 %copy.10 = f32[2,131072]{1,0:T(2,128)} copy(f32[2,131072]{1,0:T(2,128)S(1)} %bitcast.11) | data formatting | bytes 2097152

commit v6 on v5

--- a/solution.py
+++ b/solution.py
@@ -106,7 +106,7 @@
                 device_id_type=pl.DeviceIdType.MESH,
             ).start()
 
-    send_in(0, sequence[24:])
+    send_in(0, [others[distance] for distance in (7, 6, 5, 4, 3, 2, 1)])
     for line in range(3):
         pl.semaphore_wait(lines.at[line], 1)
         send_in(0, sequence[16 - 8 * line : 24 - 8 * line])

time: 54.1 us -> 54.1 us (level)
  no operation moved by 1% of the time
where the time goes in v6:
time: 54.1 us; the launch traced here: 54 us
  Pallas kernels  53.1 us (98%)
  local copies, waits for them, and re-layouts  0.97 us (2%)
    pallas_call x1, Pallas kernels, run(): pl.pallas_call(kernel, out_shape=pltpu.VMEM(given.shape, jnp.float32), in...  53.1 us

profile of v6, /device:TPU:1, one launch (start us, length us, event | category | flops | bytes accessed | tf_op | source)
XLA Modules:
  0.0 54.0 jit_solution(8071741578509063129)
XLA Ops:
  0.0 53.1 %shard_map.64 = f32[32,2,32,128]{3,2,1,0:T(8,128)S(1)} custom-call(f32[32,2,32,128]{3,2,1,0:T(8,128)} %bitcast.12, f32[6,128,128]{2,1,0:T(8,128)} %gate_re_given.1, f32[6,128,128]{2,1,0:T(8,128)} %gate_im_given.1, s32[6,8]{1,0:T(8,128)} %bit_orders_given.1, s32[6,2,16]{2,1,0:T(2,128)} %bitcast.13, f32[6,16]{1,0:T(8,128)} %phase_angles_given.1), custom_call_target="tpu_custom_call" | custom-call | flops 4831838208 | bytes 4194304 | tf_op jit(solution)/shard_map/pallas_call | solution.py:240
  53.1 1.0 %copy.10 = f32[2,131072]{1,0:T(2,128)} copy(f32[2,131072]{1,0:T(2,128)S(1)} %bitcast.11) | data formatting | bytes 2097152

commit v7 on v6

--- a/solution.py
+++ b/solution.py
@@ -212,7 +212,7 @@
                             leaving[chunk, s * 16 + i, pl.ds(h * 2, 8, stride=4), :] = reals[i]
                             leaving[chunk, s * 16 + i, pl.ds(h * 2 + 1, 8, stride=4), :] = imags[i]
 
-        for other in sequence:
+        for other in sequence[:27] + [others[4]] + sequence[27:30]:
             pltpu.make_async_remote_copy(
                 src_ref=leaving.at[chunk, other],
                 dst_ref=result.at[me, chunk],

time: 54.1 us -> 54.1 us (level)
  no operation moved by 1% of the time
where the time goes in v7:
time: 54.1 us; the launch traced here: 54 us
  Pallas kernels  53.1 us (98%)
  local copies, waits for them, and re-layouts  0.97 us (2%)
    pallas_call x1, Pallas kernels, run(): pl.pallas_call(kernel, out_shape=pltpu.VMEM(given.shape, jnp.float32), in...  53.1 us

profile of v7, /device:TPU:1, one launch (start us, length us, event | category | flops | bytes accessed | tf_op | source)
XLA Modules:
  0.0 54.0 jit_solution(427264347821609254)
XLA Ops:
  0.0 53.1 %shard_map.64 = f32[32,2,32,128]{3,2,1,0:T(8,128)S(1)} custom-call(f32[32,2,32,128]{3,2,1,0:T(8,128)} %bitcast.12, f32[6,128,128]{2,1,0:T(8,128)} %gate_re_given.1, f32[6,128,128]{2,1,0:T(8,128)} %gate_im_given.1, s32[6,8]{1,0:T(8,128)} %bit_orders_given.1, s32[6,2,16]{2,1,0:T(2,128)} %bitcast.13, f32[6,16]{1,0:T(8,128)} %phase_angles_given.1), custom_call_target="tpu_custom_call" | custom-call | flops 4831838208 | bytes 4194304 | tf_op jit(solution)/shard_map/pallas_call | solution.py:240
  53.1 1.0 %copy.10 = f32[2,131072]{1,0:T(2,128)} copy(f32[2,131072]{1,0:T(2,128)S(1)} %bitcast.11) | data formatting | bytes 2097152
